TPU v7x, 32 devices: a whole 2x2x4 slice. The times are simulated.
32 devices in a mesh: ens: 2 (over y), bx: 8 (over z, x), by: 2 (over core).
Axes of the slice: x: 2, y: 2, z: 4, core: 2. Of those that a mesh axis runs over, the one named last changes fastest.
Arguments:
- nodes: bfloat16 [4096, 512], P(('ens', 'bx', 'by')), parts along dimension 0, may hold values from -6 to 6
- edges: bfloat16 [49152, 512], P(('ens', 'bx', 'by')), parts along dimension 0, may hold values from -6 to 6
- edge_cotangent: bfloat16 [49152, 512], P(('ens', 'bx', 'by')), parts along dimension 0, may hold values from -6 to 6
- node_cotangent: bfloat16 [4096, 512], P(('ens', 'bx', 'by')), parts along dimension 0, may hold values from -6 to 6
- senders: int32 [49152], P(('ens', 'bx', 'by')), parts along dimension 0, may hold values from 0 to 127, as said below
- receivers: int32 [49152], P(('ens', 'bx', 'by')), parts along dimension 0, may hold values from 0 to 127
- slots: int32 [384], P(('ens', 'bx', 'by')), parts along dimension 0, may hold values from 0 to 5, as said below
- live: int32 [384], P(('ens', 'bx', 'by')), parts along dimension 0, may hold values from 32 to 128, as said below
- w_edge: bfloat16 [512, 512], P('bx'), may hold values from -0.15625 to 0.15625
- w_send: bfloat16 [512, 512], P('bx'), may hold values from -0.15625 to 0.15625
- w_recv: bfloat16 [512, 512], P('bx'), may hold values from -0.15625 to 0.15625
- w_out: bfloat16 [512, 512], P('bx'), may hold values from -0.25 to 0.25
- bias: float32 [512], replicated, may hold values from -3 to 3
Outputs:
- grad_edges: bfloat16 [49152, 512], P(('ens', 'bx', 'by')), parts along dimension 0
- grad_nodes: bfloat16 [4096, 512], P(('ens', 'bx', 'by')), parts along dimension 0
There are 2 independent parts, one for each index of `ens`. A program takes and returns all parts, laid end to end along the dimension named above; an argument that names none is the same for every part. Nothing has to cross between parts.
Inputs may be any that keep to these rules, and one draw needn't show every extreme that they name: `senders`: in a block of source s, every row's sender (padded rows too) is below 128 for s = 0, below 32 for s = 1, 2, 3 and below 16 for s = 4, 5. `slots`: of the 12 blocks of each patch, exactly two take each of the sources 0 to 5. `live`: the blocks of source 0 of every patch are full.
All inputs are finite; a program needn't handle non-finite values.
Results may differ from a plain program's by a relative error of at most 0.0055.
Values may be sent and summed in bfloat16 or wider, within the bound.
A program may use at most 64 MiB of HBM per device.

v0:
```python
import jax
import jax.numpy as jnp
from jax import lax
from jax.sharding import PartitionSpec as P

COARSE = 16


def shifted(value, axis, steps):
    count = lax.axis_size(axis)
    pairs = [(source, (source + steps) % count) for source in range(count)]
    return lax.ppermute(value, axis, pairs)


def from_partner(value, axis, apart):
    mask = 2**apart
    pairs = [(source, source ^ mask) for source in range(lax.axis_size(axis))]
    return lax.ppermute(value, axis, pairs)


def silu_slope(pre_act):
    sigma = jax.nn.sigmoid(pre_act)
    return sigma * (1.0 + pre_act * (1.0 - sigma))


def per_device(
    nodes,
    edges,
    edge_cotangent,
    node_cotangent,
    senders,
    receivers,
    slots,
    live,
    w_edge,
    w_send,
    w_recv,
    w_out,
    bias,
):
    w_edge, w_send, w_recv, w_out = (
        lax.all_gather(w_edge, "bx", axis=0, tiled=True),
        lax.all_gather(w_send, "bx", axis=0, tiled=True),
        lax.all_gather(w_recv, "bx", axis=0, tiled=True),
        lax.all_gather(w_out, "bx", axis=0, tiled=True),
    )
    node_dev = nodes.shape[0]
    rim_width = node_dev // 4
    edge_count = edges.shape[0]
    block_rows = edge_count // slots.shape[0]
    bit_count = lax.axis_size("bx").bit_length() - 1
    level_bits = (bit_count - 1, bit_count - 2)
    coarse_top = nodes[:COARSE]
    left_in = shifted(nodes[node_dev - rim_width :], "bx", 1)
    right_in = shifted(nodes[:rim_width], "bx", -1)
    core_in = from_partner(nodes[rim_width : 2 * rim_width], "by", 0)
    far_rows = [from_partner(coarse_top, "bx", level_bit) for level_bit in level_bits]
    source_table = jnp.concatenate([nodes, left_in, right_in, core_in] + far_rows, axis=0)
    table_rows = source_table.shape[0]
    starts = [
        0,
        node_dev,
        node_dev + rim_width,
        node_dev + 2 * rim_width,
        node_dev + 3 * rim_width,
        node_dev + 3 * rim_width + COARSE,
    ]
    edge_slot = jnp.repeat(slots, block_rows)
    offset = jnp.zeros((edge_count,), jnp.int32)
    for source in range(6):
        offset = offset + jnp.where(edge_slot == source, starts[source], 0).astype(jnp.int32)
    sender_index = offset + senders
    proj_send = jnp.dot(source_table, w_send, preferred_element_type=jnp.float32)
    proj_recv = jnp.dot(nodes, w_recv, preferred_element_type=jnp.float32)
    pre_act = jnp.dot(edges, w_edge, preferred_element_type=jnp.float32)
    pre_act = (
        pre_act
        + jnp.take(proj_send, sender_index, axis=0)
        + jnp.take(proj_recv, receivers, axis=0)
        + bias
    )
    in_block = jnp.arange(edge_count, dtype=jnp.int32) % block_rows
    live_mask = (in_block < jnp.repeat(live, block_rows)).astype(jnp.float32)
    grad_msg = (
        (
            edge_cotangent.astype(jnp.float32)
            + jnp.take(node_cotangent, receivers, axis=0).astype(jnp.float32)
        )
        * live_mask[:, None]
    ).astype(jnp.bfloat16)
    grad_act = jnp.dot(grad_msg, w_out.T, preferred_element_type=jnp.float32)
    grad_pre = (grad_act * silu_slope(pre_act)).astype(jnp.bfloat16)
    grad_edges = (
        edge_cotangent.astype(jnp.float32)
        + jnp.dot(grad_pre, w_edge.T, preferred_element_type=jnp.float32)
    ).astype(jnp.bfloat16)
    send_onehot = (
        sender_index[:, None] == jnp.arange(table_rows, dtype=jnp.int32)[None, :]
    ).astype(jnp.bfloat16)
    recv_onehot = (receivers[:, None] == jnp.arange(node_dev, dtype=jnp.int32)[None, :]).astype(
        jnp.bfloat16
    )
    sender_sums = lax.dot_general(
        send_onehot, grad_pre, (((0,), (0,)), ((), ())), preferred_element_type=jnp.float32
    )
    recv_sums = lax.dot_general(
        recv_onehot, grad_pre, (((0,), (0,)), ((), ())), preferred_element_type=jnp.float32
    )
    back_first = sender_sums[node_dev : node_dev + rim_width]
    back_second = sender_sums[node_dev + rim_width : node_dev + 2 * rim_width]
    back_core = sender_sums[node_dev + 2 * rim_width : node_dev + 3 * rim_width]
    back_far = [sender_sums[starts[4 + level] : starts[4 + level] + COARSE] for level in range(2)]
    from_right = shifted(back_first.astype(jnp.bfloat16), "bx", -1).astype(back_first.dtype)
    from_left = shifted(back_second.astype(jnp.bfloat16), "bx", 1).astype(back_second.dtype)
    from_core = from_partner(back_core.astype(jnp.bfloat16), "by", 0).astype(back_core.dtype)
    returned = [
        from_partner(piece.astype(jnp.bfloat16), "bx", level_bit).astype(piece.dtype)
        for piece, level_bit in zip(back_far, level_bits)
    ]
    coarse_got = returned[0] + returned[1]
    own_sums = sender_sums[:node_dev]
    own_sums = own_sums.at[node_dev - rim_width :].add(from_right)
    own_sums = own_sums.at[:rim_width].add(from_left)
    own_sums = own_sums.at[rim_width : 2 * rim_width].add(from_core)
    own_sums = own_sums.at[:COARSE].add(coarse_got)
    grad_nodes = node_cotangent.astype(jnp.float32)
    grad_nodes = grad_nodes + jnp.dot(
        own_sums.astype(jnp.bfloat16), w_send.T, preferred_element_type=jnp.float32
    )
    grad_nodes = grad_nodes + jnp.dot(
        recv_sums.astype(jnp.bfloat16), w_recv.T, preferred_element_type=jnp.float32
    )
    return (grad_edges, grad_nodes.astype(jnp.bfloat16))


def solution(mesh):
    in_specs = (
        P(("ens", "bx", "by"), None),
        P(("ens", "bx", "by"), None),
        P(("ens", "bx", "by"), None),
        P(("ens", "bx", "by"), None),
        P(("ens", "bx", "by")),
        P(("ens", "bx", "by")),
        P(("ens", "bx", "by")),
        P(("ens", "bx", "by")),
        P("bx", None),
        P("bx", None),
        P("bx", None),
        P("bx", None),
        P(),
    )
    out_specs = (P(("ens", "bx", "by"), None), P(("ens", "bx", "by"), None))
    return jax.shard_map(
        per_device, mesh=mesh, in_specs=in_specs, out_specs=out_specs, check_vma=False
    )
```

profile of v0, /device:TPU:0, one launch (start us, length us, event | category | flops | bytes accessed | tf_op | source)
XLA Modules:
  0.0 188.4 jit_solution(14106446888956700419)
XLA Ops:
  0.6 0.0 copy-start
  0.7 0.9 slice.115
  1.5 3.0 %collective-permute-start.4 = (bf16[16,512]{1,0:T(8,128)(2,1)S(1)}, bf16[16,512]{1,0:T(8,128)(2,1)S(1)}, u32[]{:S(2)}, u32[]{:S(2)}) collective-permute-start(bf16[16,512]{1,0:T(8,128)(2,1)S(1)} %slice.115), channel_id=1, source_target_pairs={{0,4},{2,6},{4,0},{6,2},{8,12},{10,14},{12,8},{14,10},{1,5},{3,7},... | collective-permute-start | bytes 49160 | tf_op jit(solution)/shard_map/ppermute | solution.py:18
  4.5 2.6 %collective-permute-start.3 = (bf16[16,512]{1,0:T(8,128)(2,1)S(1)}, bf16[16,512]{1,0:T(8,128)(2,1)}, u32[]{:S(2)}, u32[]{:S(2)}) collective-permute-start(bf16[16,512]{1,0:T(8,128)(2,1)S(1)} %slice.115), channel_id=1, source_target_pairs={{0,8},{2,10},{4,12},{6,14},{8,0},{10,2},{12,4},{14,6},{1,9},{3,11}... | collective-permute-start | bytes 49160 | tf_op jit(solution)/shard_map/ppermute | solution.py:18
  7.1 0.8 fusion.31
  7.9 0.1 collective-permute-start.2
  8.0 1.2 collective-permute-start.1
  9.2 0.9 collective-permute-start
  10.1 0.9 constant_dynamic-update-slice_fusion.5
  11.0 0.7 fusion.27
  11.7 0.7 compare_select_fusion.1
  12.3 1.3 compare_and_fusion
  13.6 1.4 fusion.23
  15.0 31.8 %all_gather.13 = bf16[512,512]{1,0:T(8,128)(2,1)S(1)} all-gather(bf16[64,512]{1,0:T(8,128)(2,1)} %param.29), channel_id=1, replica_groups=mesh['ens'=2,'bx'=8,'by'=2] {'bx'}, dimensions={0}, use_global_device_ids=true | all-gather | bytes 589824 | tf_op jit(solution)/shard_map/all_gather | solution.py:42
  46.8 31.5 %all_gather.14 = bf16[512,512]{1,0:T(8,128)(2,1)S(1)} all-gather(bf16[64,512]{1,0:T(8,128)(2,1)} %param.30), channel_id=1, replica_groups=mesh['ens'=2,'bx'=8,'by'=2] {'bx'}, dimensions={0}, use_global_device_ids=true | all-gather | bytes 589824 | tf_op jit(solution)/shard_map/all_gather | solution.py:43
  78.3 31.4 %all_gather.15 = bf16[512,512]{1,0:T(8,128)(2,1)S(1)} all-gather(bf16[64,512]{1,0:T(8,128)(2,1)} %param.31), channel_id=1, replica_groups=mesh['ens'=2,'bx'=8,'by'=2] {'bx'}, dimensions={0}, use_global_device_ids=true | all-gather | bytes 589824 | tf_op jit(solution)/shard_map/all_gather | solution.py:44
  109.7 1.1 fusion.35
  110.8 33.2 %all_gather.12 = bf16[512,512]{1,0:T(8,128)(2,1)} all-gather(bf16[64,512]{1,0:T(8,128)(2,1)S(1)} %copy-done.6), channel_id=1, replica_groups=mesh['ens'=2,'bx'=8,'by'=2] {'bx'}, dimensions={0}, use_global_device_ids=true | all-gather | bytes 589824 | tf_op jit(solution)/shard_map/all_gather | solution.py:45
  144.0 2.6 %fusion.33 = f32[1536,512]{1,0:T(8,128)} fusion(bf16[1536,512]{1,0:T(8,128)(2,1)S(1)} %copy-done, bf16[512,512]{1,0:T(8,128)(2,1)S(1)} %all_gather.13), kind=kOutput, calls=%fused_computation.66 | convolution fusion | flops 805306368 | bytes 5242880 | tf_op jit(solution)/shard_map/dot_general | solution.py:75
  146.7 5.4 %gather_fusion = bf16[1536,512]{1,0:T(8,128)(2,1)} fusion(bf16[128,512]{1,0:T(8,128)(2,1)S(1)} %copy-done.1, s32[2048]{0:T(1024)S(1)} %get-tuple-element.63), kind=kCustom, calls=%fused_computation | custom fusion | bytes 3151872 | tf_op jit(solution)/shard_map/jit(_take)/gather | solution.py:87
  152.1 4.9 %gather_fusion.2 = f32[1536,512]{1,0:T(8,128)} fusion(f32[128,512]{1,0:T(8,128)S(1)} %fusion.35, s32[2048]{0:T(1024)S(1)} %get-tuple-element.63), kind=kCustom, calls=%fused_computation.2 | custom fusion | bytes 6297600 | tf_op jit(solution)/shard_map/jit(_take)/gather | solution.py:79
  157.0 0.0 collective-permute-done
  157.1 0.0 collective-permute-done.1
  157.1 0.0 collective-permute-done.2
  157.1 0.0 collective-permute-done.3
  157.1 0.7 constant_dynamic-update-slice_fusion.1
  157.8 0.0 collective-permute-done.4
  157.8 0.3 fusion.34
  158.1 0.0 copy-start.7
  158.2 0.0 copy-start.11
  158.2 5.0 %gather_fusion.1 = f32[1536,512]{1,0:T(8,128)} fusion(f32[256,512]{1,0:T(8,128)S(1)} %fusion.34, s32[2048]{0:T(1024)S(1)} %get-tuple-element.62), kind=kCustom, calls=%fused_computation.1 | custom fusion | bytes 6297600 | tf_op jit(solution)/shard_map/jit(_take)/gather | solution.py:78
  163.2 0.0 copy-start.10
  163.2 7.1 %fusion.2 = bf16[1536,512]{1,0:T(8,128)(2,1)S(1)} fusion(f32[1536,512]{1,0:T(8,128)} %gather_fusion.2, f32[1536,512]{1,0:T(8,128)} %fusion.33, f32[1536,512]{1,0:T(8,128)} %gather_fusion.1, bf16[512,512]{1,0:T(8,128)(2,1)} %all_gather.12, bf16[1536,512]{1,0:T(8,128)(2,1)} %param.23, f32[512]{0:T(512)S(1)} %copy-done.11, f32[1536]{0:T(1024)S(1)} %copy-done.7, ...), kind=kOutput, calls=%fused_computation.8 | convolution fusion | flops 821035008 | bytes 14691328 | tf_op jit(solution)/shard_map/dot_general | solution.py:91
  170.4 0.9 fusion.32
  171.3 0.0 copy-start.5
  171.3 2.2 %fusion.3 = bf16[1536,512]{1,0:T(8,128)(2,1)} fusion(bf16[1536,512]{1,0:T(8,128)(2,1)S(1)} %fusion.2, bf16[512,512]{1,0:T(8,128)(2,1)S(1)} %copy-done.3, bf16[1536,512]{1,0:T(8,128)(2,1)S(1)} %copy-done.10), kind=kOutput, calls=%fused_computation.9 | convolution fusion | flops 807665664 | bytes 5242880 | tf_op jit(solution)/shard_map/dot_general | solution.py:95
  173.5 4.7 %collective-permute-start.5 = (bf16[32,512]{1,0:T(8,128)(2,1)S(1)}, bf16[32,512]{1,0:T(8,128)(2,1)S(1)}, u32[]{:S(2)}, u32[]{:S(2)}) collective-permute-start(bf16[32,512]{1,0:T(8,128)(2,1)S(1)} %get-tuple-element.56), channel_id=1, source_target_pairs={{0,14},{2,0},{4,2},{6,4},{8,6},{10,8},{12,10},{14,12},{1,15},{3,1}... | collective-permute-start | bytes 98312 | tf_op jit(solution)/shard_map/ppermute | solution.py:12
  178.2 0.0 collective-permute-start.8
  178.2 0.0 collective-permute-start.9
  178.2 0.1 collective-permute-start.7
  178.3 1.1 collective-permute-start.6
  179.4 0.4 collective-permute-done.5
  179.8 5.2 %collective-permute-done.6 = bf16[32,512]{1,0:T(8,128)(2,1)S(1)} collective-permute-done((bf16[32,512]{1,0:T(8,128)(2,1)S(1)}, bf16[32,512]{1,0:T(8,128)(2,1)S(1)}, u32[]{:S(2)}, u32[]{:S(2)}) %collective-permute-start.6) | collective-permute-done | bytes 32800 | tf_op jit(solution)/shard_map/ppermute | solution.py:12
  184.9 0.0 collective-permute-done.7
  185.0 0.0 collective-permute-done.8
  185.0 0.0 collective-permute-done.9
  185.0 0.3 convolution_add_fusion.1
  185.3 3.0 %fusion.9 = bf16[128,512]{1,0:T(8,128)(2,1)} fusion(f32[128,512]{1,0:T(8,128)S(1)} %convolution_add_fusion.1, bf16[512,512]{1,0:T(8,128)(2,1)S(1)} %all_gather.15, bf16[1536,512]{1,0:T(8,128)(2,1)} %copy-done.4, s32[1536]{0:T(1024)S(1)} %copy-done.5), kind=kOutput, calls=%fused_computation.17 | convolution fusion | flops 268828672 | bytes 2496512 | tf_op jit(solution)/shard_map/dot_general | solution.py:130
  (32 shorter events, 0.1 us)
Async XLA Ops:
  0.6 143.4 %copy-start = (bf16[1536,512]{1,0:T(8,128)(2,1)S(1)}, bf16[1536,512]{1,0:T(8,128)(2,1)}, u32[]{:S(2)}) copy-start(bf16[1536,512]{1,0:T(8,128)(2,1)} %param.22) | copy-start | bytes 4718596
  0.6 110.2 %copy-start.6 = (bf16[64,512]{1,0:T(8,128)(2,1)S(1)}, bf16[64,512]{1,0:T(8,128)(2,1)}, u32[]{:S(2)}) copy-start(bf16[64,512]{1,0:T(8,128)(2,1)} %param.32) | copy-start | bytes 196612
  1.5 156.3 %collective-permute-start.4 = (bf16[16,512]{1,0:T(8,128)(2,1)S(1)}, bf16[16,512]{1,0:T(8,128)(2,1)S(1)}, u32[]{:S(2)}, u32[]{:S(2)}) collective-permute-start(bf16[16,512]{1,0:T(8,128)(2,1)S(1)} %slice.115), channel_id=1, source_target_pairs={{0,4},{2,6},{4,0},{6,2},{8,12},{10,14},{12,8},{14,10},{1,5},{3,7},... | collective-permute-start | bytes 49160 | tf_op jit(solution)/shard_map/ppermute | solution.py:18
  4.5 152.6 %collective-permute-start.3 = (bf16[16,512]{1,0:T(8,128)(2,1)S(1)}, bf16[16,512]{1,0:T(8,128)(2,1)}, u32[]{:S(2)}, u32[]{:S(2)}) collective-permute-start(bf16[16,512]{1,0:T(8,128)(2,1)S(1)} %slice.115), channel_id=1, source_target_pairs={{0,8},{2,10},{4,12},{6,14},{8,0},{10,2},{12,4},{14,6},{1,9},{3,11}... | collective-permute-start | bytes 49160 | tf_op jit(solution)/shard_map/ppermute | solution.py:18
  7.9 149.2 %collective-permute-start.2 = (bf16[32,512]{1,0:T(8,128)(2,1)S(1)}, bf16[32,512]{1,0:T(8,128)(2,1)S(1)}, u32[]{:S(2)}, u32[]{:S(2)}) collective-permute-start(bf16[32,512]{1,0:T(8,128)(2,1)S(1)} %get-tuple-element.57), channel_id=1, source_target_pairs={{0,1},{1,0},{2,3},{3,2},{4,5},{5,4},{6,7},{7,6},{8,9},{9,8},{10,11... | collective-permute-start | bytes 98312 | tf_op jit(solution)/shard_map/ppermute | solution.py:18
  8.0 149.1 %collective-permute-start.1 = (bf16[32,512]{1,0:T(8,128)(2,1)S(1)}, bf16[32,512]{1,0:T(8,128)(2,1)S(1)}, u32[]{:S(2)}, u32[]{:S(2)}) collective-permute-start(bf16[32,512]{1,0:T(8,128)(2,1)S(1)} %get-tuple-element.58), channel_id=1, source_target_pairs={{0,14},{2,0},{4,2},{6,4},{8,6},{10,8},{12,10},{14,12},{1,15},{3,1}... | collective-permute-start | bytes 98312 | tf_op jit(solution)/shard_map/ppermute | solution.py:12
  9.2 147.9 %collective-permute-start = (bf16[32,512]{1,0:T(8,128)(2,1)S(1)}, bf16[32,512]{1,0:T(8,128)(2,1)S(1)}, u32[]{:S(2)}, u32[]{:S(2)}) collective-permute-start(bf16[32,512]{1,0:T(8,128)(2,1)S(1)} %get-tuple-element.59), channel_id=1, source_target_pairs={{0,2},{2,4},{4,6},{6,8},{8,10},{10,12},{12,14},{14,0},{1,3},{3,5},... | collective-permute-start | bytes 98312 | tf_op jit(solution)/shard_map/ppermute | solution.py:12
  46.8 99.9 %copy-start.2 = (bf16[512,512]{1,0:T(8,128)(2,1)}, bf16[512,512]{1,0:T(8,128)(2,1)S(1)}, u32[]{:S(2)}) copy-start(bf16[512,512]{1,0:T(8,128)(2,1)S(1)} %all_gather.13) | copy-start | bytes 1572868
  144.0 2.7 %copy-start.1 = (bf16[128,512]{1,0:T(8,128)(2,1)S(1)}, bf16[128,512]{1,0:T(8,128)(2,1)}, u32[]{:S(2)}) copy-start(bf16[128,512]{1,0:T(8,128)(2,1)} %param.24) | copy-start | bytes 393220
  158.1 5.1 %copy-start.7 = (f32[1536]{0:T(1024)S(1)}, f32[1536]{0:T(1024)}, u32[]{:S(2)}) copy-start(f32[1536]{0:T(1024)} %get-tuple-element.64) | copy-start | bytes 18436
  158.1 5.0 %copy-start.8 = (pred[1536]{0:T(1024)(128)(4,1)S(1)}, pred[1536]{0:T(1024)(128)(4,1)}, u32[]{:S(2)}) copy-start(pred[1536]{0:T(1024)(128)(4,1)} %get-tuple-element.50) | copy-start | bytes 4612
  158.2 5.0 %copy-start.9 = (pred[1536]{0:T(1024)(128)(4,1)S(1)}, pred[1536]{0:T(1024)(128)(4,1)}, u32[]{:S(2)}) copy-start(pred[1536]{0:T(1024)(128)(4,1)} %get-tuple-element.65) | copy-start | bytes 4612
  158.2 5.0 %copy-start.11 = (f32[512]{0:T(512)S(1)}, f32[512]{0:T(512)}, u32[]{:S(2)}) copy-start(f32[512]{0:T(512)} %param.33) | copy-start | bytes 6148
  163.2 8.1 %copy-start.3 = (bf16[512,512]{1,0:T(8,128)(2,1)S(1)}, bf16[512,512]{1,0:T(8,128)(2,1)}, u32[]{:S(2)}) copy-start(bf16[512,512]{1,0:T(8,128)(2,1)} %copy-done.2) | copy-start | bytes 1572868
  163.2 8.1 %copy-start.10 = (bf16[1536,512]{1,0:T(8,128)(2,1)S(1)}, bf16[1536,512]{1,0:T(8,128)(2,1)}, u32[]{:S(2)}) copy-start(bf16[1536,512]{1,0:T(8,128)(2,1)} %param.23) | copy-start | bytes 4718596
  170.4 3.1 %copy-start.4 = (bf16[1536,512]{1,0:T(8,128)(2,1)}, bf16[1536,512]{1,0:T(8,128)(2,1)S(1)}, u32[]{:S(2)}) copy-start(bf16[1536,512]{1,0:T(8,128)(2,1)S(1)} %fusion.2) | copy-start | bytes 4718596
  171.3 14.0 %copy-start.5 = (s32[1536]{0:T(1024)S(1)}, s32[1536]{0:T(1024)}, u32[]{:S(2)}) copy-start(s32[1536]{0:T(1024)} %param.26) | copy-start | bytes 18436
  173.5 6.3 %collective-permute-start.5 = (bf16[32,512]{1,0:T(8,128)(2,1)S(1)}, bf16[32,512]{1,0:T(8,128)(2,1)S(1)}, u32[]{:S(2)}, u32[]{:S(2)}) collective-permute-start(bf16[32,512]{1,0:T(8,128)(2,1)S(1)} %get-tuple-element.56), channel_id=1, source_target_pairs={{0,14},{2,0},{4,2},{6,4},{8,6},{10,8},{12,10},{14,12},{1,15},{3,1}... | collective-permute-start | bytes 98312 | tf_op jit(solution)/shard_map/ppermute | solution.py:12
  178.2 6.8 %collective-permute-start.8 = (bf16[16,512]{1,0:T(8,128)(2,1)S(1)}, bf16[16,512]{1,0:T(8,128)(2,1)S(1)}, u32[]{:S(2)}, u32[]{:S(2)}) collective-permute-start(bf16[16,512]{1,0:T(8,128)(2,1)S(1)} %get-tuple-element.52), channel_id=1, source_target_pairs={{0,8},{2,10},{4,12},{6,14},{8,0},{10,2},{12,4},{14,6},{1,9},{3,11}... | collective-permute-start | bytes 49160 | tf_op jit(solution)/shard_map/ppermute | solution.py:18
  178.2 6.8 %collective-permute-start.9 = (bf16[16,512]{1,0:T(8,128)(2,1)S(1)}, bf16[16,512]{1,0:T(8,128)(2,1)S(1)}, u32[]{:S(2)}, u32[]{:S(2)}) collective-permute-start(bf16[16,512]{1,0:T(8,128)(2,1)S(1)} %get-tuple-element.53), channel_id=1, source_target_pairs={{0,4},{2,6},{4,0},{6,2},{8,12},{10,14},{12,8},{14,10},{1,5},{3,7},... | collective-permute-start | bytes 49160 | tf_op jit(solution)/shard_map/ppermute | solution.py:18
  178.2 6.8 %collective-permute-start.7 = (bf16[32,512]{1,0:T(8,128)(2,1)S(1)}, bf16[32,512]{1,0:T(8,128)(2,1)S(1)}, u32[]{:S(2)}, u32[]{:S(2)}) collective-permute-start(bf16[32,512]{1,0:T(8,128)(2,1)S(1)} %get-tuple-element.54), channel_id=1, source_target_pairs={{0,1},{1,0},{2,3},{3,2},{4,5},{5,4},{6,7},{7,6},{8,9},{9,8},{10,11... | collective-permute-start | bytes 98312 | tf_op jit(solution)/shard_map/ppermute | solution.py:18
  178.3 6.7 %collective-permute-start.6 = (bf16[32,512]{1,0:T(8,128)(2,1)S(1)}, bf16[32,512]{1,0:T(8,128)(2,1)S(1)}, u32[]{:S(2)}, u32[]{:S(2)}) collective-permute-start(bf16[32,512]{1,0:T(8,128)(2,1)S(1)} %get-tuple-element.55), channel_id=1, source_target_pairs={{0,2},{2,4},{4,6},{6,8},{8,10},{10,12},{12,14},{14,0},{1,3},{3,5},... | collective-permute-start | bytes 98312 | tf_op jit(solution)/shard_map/ppermute | solution.py:12
where the time goes:
time: 189 us; the launch traced here: 188 us
  blocking collectives  128 us (68%)
  local copies, waits for them, and re-layouts  18.7 us (10%)
  matrix products  17.6 us (9%)
  starting transfers between devices  13.6 us (7%)
  waiting for transfers between devices  5.52 us (3%)
  other arithmetic  4.08 us (2%)
    all_gather x1, blocking collectives, per_device(): lax.all_gather(w_out, 'bx', axis=0, tiled=True)  33.2 us
    all_gather x1, blocking collectives, per_device(): lax.all_gather(w_edge, 'bx', axis=0, tiled=True)  31.8 us
    all_gather x1, blocking collectives, per_device(): lax.all_gather(w_send, 'bx', axis=0, tiled=True)  31.5 us
    all_gather x1, blocking collectives, per_device(): lax.all_gather(w_recv, 'bx', axis=0, tiled=True)  31.4 us
    ppermute x4, starting transfers between devices, shifted(): return lax.ppermute(value, axis, pairs)  7.87 us
    dot_general x1, matrix products, per_device(): grad_act = jnp.dot(grad_msg, w_out.T, preferred_element_type=jnp.float32)  7.12 us
    ppermute x6, starting transfers between devices, from_partner(): return lax.ppermute(value, axis, pairs)  5.75 us
    ppermute x4, waiting for transfers between devices, shifted(): return lax.ppermute(value, axis, pairs)  5.51 us
  transfers between devices with their start and end apart: 10, of which 2 were waited for; matrix products, arithmetic and copies ran while one was open for 11% of the time, Pallas kernels for 0%

commit v1 on v0

v1 whole, which is shorter than its diff:
```python
import functools

import jax
import jax.numpy as jnp
from jax import lax
from jax.experimental import pallas as pl
from jax.experimental.pallas import tpu as pltpu
from jax.sharding import PartitionSpec as P

COARSE = 16
MESH = pl.DeviceIdType.MESH
NN = (((1,), (0,)), ((), ()))
NT = (((1,), (1,)), ((), ()))


def dot(a, b, dims=NN):
    return lax.dot_general(a, b, dims, preferred_element_type=jnp.float32)


def flip(index, apart):
    return index + apart * (1 - 2 * ((index // apart) % 2))


def kernel(
    cfg,
    slots_ref,
    live_ref,
    senders_ref,
    receivers_ref,
    bias_ref,
    nodes_hbm,
    edges_hbm,
    cot_hbm,
    ncot_hbm,
    wout_hbm,
    wedge_hbm,
    wsend_hbm,
    wrecv_hbm,
    gedges_hbm,
    gnodes_ref,
    wall,
    table,
    edges_v,
    cot_v,
    ncot_v,
    oh,
    oht,
    gmsg,
    gact,
    pre,
    proj,
    gpre,
    sums,
    back_out,
    back_in,
    out_v,
    local_sem,
    out_sem,
    send_sem,
    recv_sem,
):
    n_bx, gather, nz, shard_rows, chunk = cfg
    node_dev = ncot_v.shape[0]
    rim = node_dev // 4
    block = senders_ref.shape[1]
    blocks = senders_ref.shape[0]
    rows = edges_v.shape[0]
    ens, bx, by = lax.axis_index("ens"), lax.axis_index("bx"), lax.axis_index("by")
    z, x = bx // 2, bx % 2

    def local(source, target, number):
        return pltpu.make_async_copy(source, target, local_sem.at[number])

    weights = (wout_hbm, wedge_hbm, wsend_hbm, wrecv_hbm)
    w_copies = []
    for number, ref in enumerate(weights):
        target = wall.at[number, z, x] if gather else wall.at[number]
        w_copies.append(local(ref, target, number))
    nodes_copy = local(nodes_hbm, table.at[pl.ds(0, node_dev)], 4)
    ncot_copy = local(ncot_hbm, ncot_v, 5)
    cot_copy = local(cot_hbm, cot_v, 6)
    edges_copy = local(edges_hbm, edges_v, 7)
    for copy in [nodes_copy] + w_copies + [ncot_copy, cot_copy, edges_copy]:
        copy.start()

    right = (ens, (bx + 1) % n_bx, by)
    left = (ens, (bx + n_bx - 1) % n_bx, by)
    core = (ens, bx, 1 - by)
    far = [(ens, flip(bx, n_bx // 2), by), (ens, flip(bx, n_bx // 4), by)]
    x_peer = (ens, z * 2 + 1 - x, by)
    y_peer = (1 - ens, bx, by)
    greeted = [right, left, core] + far
    if gather:
        greeted += [(ens, ((z + dz) % nz) * 2 + x, by) for dz in range(1, nz)]
        greeted += [x_peer, y_peer]

    barrier = pltpu.get_barrier_semaphore()
    for device in greeted:
        pl.semaphore_signal(barrier, inc=1, device_id=device, device_id_type=MESH)
    pl.semaphore_wait(barrier, len(greeted))

    used = [0]
    sent = []

    def message(source, target, device, incoming):
        number = used[0]
        used[0] += 1
        out = pltpu.make_async_remote_copy(
            src_ref=source,
            dst_ref=target,
            send_sem=send_sem.at[number],
            recv_sem=recv_sem.at[number],
            device_id=device,
            device_id_type=MESH,
        )
        out.start()
        sent.append(out)
        return pltpu.make_async_remote_copy(
            src_ref=incoming,
            dst_ref=incoming,
            send_sem=send_sem.at[number],
            recv_sem=recv_sem.at[number],
            device_id=device,
            device_id_type=MESH,
        )

    nodes_copy.wait()
    pieces = [
        (node_dev - rim, rim, right),
        (0, rim, left),
        (rim, rim, core),
        (0, COARSE, far[0]),
        (0, COARSE, far[1]),
    ]
    node_msgs = []
    place = node_dev
    for start, size, device in pieces:
        target = table.at[pl.ds(place, size)]
        node_msgs.append(message(table.at[pl.ds(start, size)], target, device, target))
        place += size

    def part_a(zz, xx, e, b):
        size = shard_rows // 4
        start = pl.multiple_of((2 * e + b) * size, size)
        return wall.at[pl.ds(0, 2), zz, xx, pl.ds(start, size)]

    def part_b(zz, xx, e, b):
        size = shard_rows // 2
        start = pl.multiple_of(b * size, size)
        return wall.at[pl.ds(2, 2), zz, xx, pl.ds(start, size)]

    def z_sends(part):
        got = []
        own = part(z, x, ens, by)
        for dz in range(1, nz):
            incoming = part((z - dz + nz) % nz, x, ens, by)
            got.append(message(own, own, (ens, ((z + dz) % nz) * 2 + x, by), incoming))
        return got

    def forward(part, dz, xx, e, b, device, arrives):
        zz = (z - dz + nz) % nz
        source = part(zz, xx, e, b)
        return message(source, source, device, part(zz, *arrives))

    def to_x(part, dz):
        return forward(part, dz, x, ens, by, x_peer, (1 - x, ens, by))

    def to_y(part, dz, xx):
        return forward(part, dz, xx, ens, by, y_peer, (xx, 1 - ens, by))

    def to_core(part, dz, xx, e):
        return forward(part, dz, xx, e, by, core, (xx, e, 1 - by))

    def prepare(first, last):
        @pl.loop(first, last)
        def _(number):
            row = pl.multiple_of(number * block, block)
            here = pl.ds(row, block)
            slot = slots_ref[number]
            offset = jnp.where(slot == 0, 0, node_dev)
            offset = offset + jnp.where(slot == 2, rim, 0)
            offset = offset + jnp.where(slot == 3, 2 * rim, 0)
            offset = offset + jnp.where(slot >= 4, 3 * rim, 0)
            offset = offset + jnp.where(slot == 5, COARSE, 0)
            sender = senders_ref[pl.ds(number, 1), :] + offset
            receiver = receivers_ref[pl.ds(number, 1), :]
            lines = lax.broadcasted_iota(jnp.int32, (2 * node_dev, block), 0)
            hot_s = jnp.where(lines == sender, 1.0, 0.0)
            lines = lax.broadcasted_iota(jnp.int32, (node_dev, block), 0)
            hot_r = jnp.where(lines == receiver, 1.0, 0.0)
            hot = jnp.concatenate([hot_s, hot_r], axis=0)
            oht[:, here] = hot.astype(jnp.bfloat16)
            turned = hot.T.astype(jnp.bfloat16)
            oh[here, :] = turned
            ncot = dot(turned[:, 2 * node_dev :], ncot_v[...])
            total = cot_v[here, :].astype(jnp.float32) + ncot
            lines = lax.broadcasted_iota(jnp.int32, total.shape, 0)
            total = jnp.where(lines < live_ref[number], total, 0.0)
            gmsg[here, :] = total.astype(jnp.bfloat16)

    third = blocks // 3
    for copy in w_copies:
        copy.wait()
    if gather:
        a_z = z_sends(part_a)
        a_x = [to_x(part_a, 0)]
        b_z = z_sends(part_b)
        b_x = [to_x(part_b, 0)]
    ncot_copy.wait()
    cot_copy.wait()
    prepare(0, third)
    a_y, a_c, a_c2, b_c = [], [], [], []
    if gather:
        for dz in range(1, nz):
            a_z[dz - 1].wait_recv()
            a_x.append(to_x(part_a, dz))
            a_y.append((dz, x, to_y(part_a, dz, x)))
            a_c.append(to_core(part_a, dz, x, ens))
        prepare(third, 2 * third)
        for dz in range(nz):
            a_x[dz].wait_recv()
            a_y.append((dz, 1 - x, to_y(part_a, dz, 1 - x)))
            a_c.append(to_core(part_a, dz, 1 - x, ens))
        for dz in range(1, nz):
            b_z[dz - 1].wait_recv()
            b_x.append(to_x(part_b, dz))
            b_c.append(to_core(part_b, dz, x, ens))
        prepare(2 * third, blocks)
        for dz, xx, arrival in a_y:
            arrival.wait_recv()
            a_c2.append(to_core(part_a, dz, xx, 1 - ens))
        for dz in range(nz):
            b_x[dz].wait_recv()
            b_c.append(to_core(part_b, dz, 1 - x, ens))
        for arrival in a_c + a_c2:
            arrival.wait_recv()
    else:
        prepare(third, blocks)

    def weight(number):
        value = wall[number]
        return value.reshape(-1, value.shape[-1])

    edges_copy.wait()

    @pl.loop(0, rows // chunk)
    def _(number):
        here = pl.ds(pl.multiple_of(number * chunk, chunk), chunk)
        gact[here, :] = dot(gmsg[here, :], weight(0), NT)
        pre[here, :] = dot(edges_v[here, :], weight(1)) + bias_ref[...]

    for arrival in b_c + node_msgs:
        arrival.wait_recv()
    proj[pl.ds(0, 2 * node_dev), :] = dot(table[...], weight(2)).astype(jnp.bfloat16)
    proj[pl.ds(2 * node_dev, node_dev), :] = dot(
        table[pl.ds(0, node_dev), :], weight(3)
    ).astype(jnp.bfloat16)

    @pl.loop(0, rows // chunk)
    def _(number):
        here = pl.ds(pl.multiple_of(number * chunk, chunk), chunk)
        act = pre[here, :] + dot(oh[here, :], proj[...])
        sigma = 0.5 + 0.5 * jnp.tanh(0.5 * act)
        slope = sigma * (1.0 + act * (1.0 - sigma))
        gpre[here, :] = (gact[here, :] * slope).astype(jnp.bfloat16)

    sums[...] = dot(oht[...], gpre[...])
    back_out[...] = sums[pl.ds(node_dev, node_dev), :].astype(jnp.bfloat16)
    backs = [(rim, left), (rim, right), (rim, core), (COARSE, far[0]), (COARSE, far[1])]
    back_msgs = []
    place = 0
    for size, device in backs:
        here = pl.ds(place, size)
        back_msgs.append(message(back_out.at[here], back_in.at[here], device, back_in.at[here]))
        place += size

    outs = []
    for number in range(rows // chunk):
        here = pl.ds(number * chunk, chunk)
        out_v[here, :] = (
            cot_v[here, :].astype(jnp.float32) + dot(gpre[here, :], weight(1), NT)
        ).astype(jnp.bfloat16)
        copy = pltpu.make_async_copy(out_v.at[here], gedges_hbm.at[here], out_sem.at[number])
        copy.start()
        outs.append(copy)

    received = dot(
        sums[pl.ds(2 * node_dev, node_dev), :].astype(jnp.bfloat16), weight(3), NT
    ) + ncot_v[...].astype(jnp.float32)
    for arrival in back_msgs:
        arrival.wait_recv()
    own = sums[pl.ds(0, node_dev), :]
    got = back_in[...].astype(jnp.float32)
    coarse = got[3 * rim : 3 * rim + COARSE] + got[3 * rim + COARSE :]
    low = own[:rim] + got[rim : 2 * rim]
    low = jnp.concatenate([low[:COARSE] + coarse, low[COARSE:]], axis=0)
    middle = own[rim : 2 * rim] + got[2 * rim : 3 * rim]
    high = own[node_dev - rim :] + got[:rim]
    own = jnp.concatenate([low, middle, own[2 * rim : node_dev - rim], high], axis=0)
    gnodes_ref[...] = (received + dot(own.astype(jnp.bfloat16), weight(2), NT)).astype(
        jnp.bfloat16
    )
    for copy in sent:
        copy.wait_send()
    for copy in outs:
        copy.wait()


def per_device(
    n_bx,
    nodes,
    edges,
    edge_cotangent,
    node_cotangent,
    senders,
    receivers,
    slots,
    live,
    w_edge,
    w_send,
    w_recv,
    w_out,
    bias,
):
    shard_rows, width = w_edge.shape
    depth = shard_rows * n_bx
    gather = shard_rows % 64 == 0 and n_bx % 2 == 0
    weights = [w_out, w_edge, w_send, w_recv]
    if not gather:
        weights = [lax.all_gather(w, "bx", axis=0, tiled=True) for w in weights]
    nz = n_bx // 2
    rows = edges.shape[0]
    blocks = slots.shape[0]
    block = rows // blocks
    node_dev = nodes.shape[0]
    chunk = rows // 3
    cfg = (n_bx, gather, nz, shard_rows, chunk)
    bf16, f32 = jnp.bfloat16, jnp.float32
    wall = (4, nz, 2, shard_rows, width) if gather else (4, depth, width)
    count = 3 * nz + 64
    smem = pl.BlockSpec(memory_space=pltpu.SMEM)
    vmem = pl.BlockSpec(memory_space=pltpu.VMEM)
    hbm = pl.BlockSpec(memory_space=pl.ANY)
    return pl.pallas_call(
        functools.partial(kernel, cfg),
        out_shape=(
            jax.ShapeDtypeStruct((rows, width), bf16),
            jax.ShapeDtypeStruct((node_dev, width), bf16),
        ),
        in_specs=[smem, smem, vmem, vmem, vmem] + [hbm] * 8,
        out_specs=(hbm, vmem),
        scratch_shapes=[
            pltpu.VMEM(wall, bf16),
            pltpu.VMEM((2 * node_dev, width), bf16),
            pltpu.VMEM((rows, width), bf16),
            pltpu.VMEM((rows, width), bf16),
            pltpu.VMEM((node_dev, width), bf16),
            pltpu.VMEM((rows, 3 * node_dev), bf16),
            pltpu.VMEM((3 * node_dev, rows), bf16),
            pltpu.VMEM((rows, width), bf16),
            pltpu.VMEM((rows, width), f32),
            pltpu.VMEM((rows, width), f32),
            pltpu.VMEM((3 * node_dev, width), bf16),
            pltpu.VMEM((rows, width), bf16),
            pltpu.VMEM((3 * node_dev, width), f32),
            pltpu.VMEM((node_dev, width), bf16),
            pltpu.VMEM((node_dev, width), bf16),
            pltpu.VMEM((rows, width), bf16),
            pltpu.SemaphoreType.DMA((8,)),
            pltpu.SemaphoreType.DMA((rows // chunk,)),
            pltpu.SemaphoreType.DMA((count,)),
            pltpu.SemaphoreType.DMA((count,)),
        ],
        compiler_params=pltpu.CompilerParams(
            collective_id=0, has_side_effects=True, vmem_limit_bytes=48 * 1024 * 1024
        ),
    )(
        slots,
        live,
        senders.reshape(blocks, block),
        receivers.reshape(blocks, block),
        bias.reshape(1, width),
        nodes,
        edges,
        edge_cotangent,
        node_cotangent,
        *weights,
    )


def solution(mesh):
    n_bx = mesh.shape["bx"]
    in_specs = (
        P(("ens", "bx", "by"), None),
        P(("ens", "bx", "by"), None),
        P(("ens", "bx", "by"), None),
        P(("ens", "bx", "by"), None),
        P(("ens", "bx", "by")),
        P(("ens", "bx", "by")),
        P(("ens", "bx", "by")),
        P(("ens", "bx", "by")),
        P("bx", None),
        P("bx", None),
        P("bx", None),
        P("bx", None),
        P(),
    )
    out_specs = (P(("ens", "bx", "by"), None), P(("ens", "bx", "by"), None))
    return jax.shard_map(
        functools.partial(per_device, n_bx),
        mesh=mesh,
        in_specs=in_specs,
        out_specs=out_specs,
        check_vma=False,
    )
```

time: 189 us -> 48.3 us (0.26)
  blocking collectives: 128 us -> 0 us
  Pallas kernels: 0 us -> 34 us
  matrix products: 17.6 us -> 0 us
  starting transfers between devices: 13.6 us -> 0 us
  waiting for transfers between devices: 5.52 us -> 0 us
  local copies, waits for them, and re-layouts: 18.7 us -> 13.2 us
  other arithmetic: 4.08 us -> 0 us
    all_gather x4 -> x0, blocking collectives: 128 us -> none  [the longest x1 33.2 us: per_device(): lax.all_gather(w_out, 'bx', axis=0, tiled=True)]
    pallas_call x0 -> x1, Pallas kernels: none -> 34 us  [per_device(): pl.pallas_call(functools.partial(kernel, cfg), out_shape=(jax.ShapeDtypeS...]
    dot_general x8 -> x0, matrix products: 17.6 us -> none  [the longest x1 7.12 us: per_device(): grad_act = jnp.dot(grad_msg, w_out.T, preferred_element_type=jnp.float32)]
    gather x3 -> x0, local copies, waits for them, and re-layouts: 15.4 us -> none  [the longest x1 5.41 us: per_device(): jnp.take(node_cotangent, receivers, axis=0).astype(jnp.float32)]
    ppermute x10 -> x0, starting transfers between devices: 13.6 us -> none  [the longest x4 7.87 us: shifted(): return lax.ppermute(value, axis, pairs)]
    unnamed x29 -> x28, local copies, waits for them, and re-layouts: 1.71 us -> 13.2 us
    ppermute x10 -> x0, waiting for transfers between devices: 5.52 us -> none  [the longest x4 5.51 us: shifted(): return lax.ppermute(value, axis, pairs)]
  transfers between devices with their start and end apart: 10 -> 0, of which waited for: 2 -> 0; matrix products, arithmetic and copies ran while one was open for 11% -> 0% of each run, Pallas kernels for 0% -> 0%
where the time goes in v1:
time: 48.3 us; the launch traced here: 47.8 us
  Pallas kernels  34 us (70%)
  local copies, waits for them, and re-layouts  13.2 us (27%)
  between operations  0.66 us (1%)
    pallas_call x1, Pallas kernels, per_device(): pl.pallas_call(functools.partial(kernel, cfg), out_shape=(jax.ShapeDtypeS...  34 us
    unnamed x28, local copies, waits for them, and re-layouts  13.2 us

profile of v1, /device:TPU:0, one launch (start us, length us, event | category | flops | bytes accessed | tf_op | source)
XLA Modules:
  0.0 47.8 jit_solution(4431438332735632050)
XLA Ops:
  0.6 0.0 copy-start
  0.6 1.4 %copy-done = bf16[1536,512]{1,0:T(8,128)(2,1)S(1)} copy-done((bf16[1536,512]{1,0:T(8,128)(2,1)S(1)}, bf16[1536,512]{1,0:T(8,128)(2,1)}, u32[]{:S(2)}) %copy-start) | copy-done | bytes 1572888
  2.0 0.0 copy-start.1
  2.0 1.4 %copy-done.1 = bf16[1536,512]{1,0:T(8,128)(2,1)S(1)} copy-done((bf16[1536,512]{1,0:T(8,128)(2,1)S(1)}, bf16[1536,512]{1,0:T(8,128)(2,1)}, u32[]{:S(2)}) %copy-start.1) | copy-done | bytes 1572888
  3.5 0.0 copy-start.2
  3.5 0.9 %copy-done.2 = bf16[128,512]{1,0:T(8,128)(2,1)S(1)} copy-done((bf16[128,512]{1,0:T(8,128)(2,1)S(1)}, bf16[128,512]{1,0:T(8,128)(2,1)}, u32[]{:S(2)}) %copy-start.2) | copy-done | bytes 131096
  4.4 0.0 copy-start.3
  4.4 0.9 %copy-done.3 = bf16[128,512]{1,0:T(8,128)(2,1)S(1)} copy-done((bf16[128,512]{1,0:T(8,128)(2,1)S(1)}, bf16[128,512]{1,0:T(8,128)(2,1)}, u32[]{:S(2)}) %copy-start.3) | copy-done | bytes 131096
  5.3 0.0 copy-start.4
  5.3 0.8 %copy-done.4 = bf16[64,512]{1,0:T(8,128)(2,1)S(1)} copy-done((bf16[64,512]{1,0:T(8,128)(2,1)S(1)}, bf16[64,512]{1,0:T(8,128)(2,1)}, u32[]{:S(2)}) %copy-start.4) | copy-done | bytes 65560
  6.1 0.0 copy-start.5
  6.1 0.8 %copy-done.5 = bf16[64,512]{1,0:T(8,128)(2,1)S(1)} copy-done((bf16[64,512]{1,0:T(8,128)(2,1)S(1)}, bf16[64,512]{1,0:T(8,128)(2,1)}, u32[]{:S(2)}) %copy-start.5) | copy-done | bytes 65560
  6.9 0.0 copy-start.6
  6.9 0.8 %copy-done.6 = bf16[64,512]{1,0:T(8,128)(2,1)S(1)} copy-done((bf16[64,512]{1,0:T(8,128)(2,1)S(1)}, bf16[64,512]{1,0:T(8,128)(2,1)}, u32[]{:S(2)}) %copy-start.6) | copy-done | bytes 65560
  7.8 0.0 copy-start.7
  7.8 0.8 %copy-done.7 = bf16[64,512]{1,0:T(8,128)(2,1)S(1)} copy-done((bf16[64,512]{1,0:T(8,128)(2,1)S(1)}, bf16[64,512]{1,0:T(8,128)(2,1)}, u32[]{:S(2)}) %copy-start.7) | copy-done | bytes 65560
  8.6 0.0 copy-start.8
  8.6 0.7 %copy-done.8 = s32[1536]{0:T(1024)S(1)} copy-done((s32[1536]{0:T(1024)S(1)}, s32[1536]{0:T(1024)}, u32[]{:S(2)}) %copy-start.8) | copy-done | bytes 6168
  9.3 0.0 copy-start.9
  9.3 0.7 %copy-done.9 = s32[1536]{0:T(1024)S(1)} copy-done((s32[1536]{0:T(1024)S(1)}, s32[1536]{0:T(1024)}, u32[]{:S(2)}) %copy-start.9) | copy-done | bytes 6168
  10.0 0.0 copy-start.10
  10.0 0.7 %copy-done.10 = f32[512]{0:T(512)S(1)} copy-done((f32[512]{0:T(512)S(1)}, f32[512]{0:T(512)}, u32[]{:S(2)}) %copy-start.10) | copy-done | bytes 2072
  10.7 0.0 copy-start.11
  10.7 0.7 %copy-done.11 = s32[12]{0:T(128)S(1)} copy-done((s32[12]{0:T(128)S(1)}, s32[12]{0:T(128)}, u32[]{:S(2)}) %copy-start.11) | copy-done | bytes 72
  11.4 0.0 copy-start.12
  11.4 0.7 %copy-done.12 = s32[12]{0:T(128)S(1)} copy-done((s32[12]{0:T(128)S(1)}, s32[12]{0:T(128)}, u32[]{:S(2)}) %copy-start.12) | copy-done | bytes 72
  12.0 34.0 %shard_map.140 = (bf16[1536,512]{1,0:T(8,128)(2,1)S(1)}, bf16[128,512]{1,0:T(8,128)(2,1)S(1)}) custom-call(s32[12]{0:T(128)S(1)} %copy-done.11, s32[12]{0:T(128)S(1)} %copy-done.12, s32[12,128]{1,0:T(8,128)S(1)} %bitcast.3, s32[12,128]{1,0:T(8,128)S(1)} %bitcast.4, f32[1,512]{1,0:T(1,128)S(1)} %bitcast.5, bf16[128,512]{1,0:T(8,128)(2,1)S(1)} %copy-done.2, ...), custom_call_target="tpu_custom_call" | custom-call | tf_op jit(solution)/shard_map/pallas_call | solution.py:344
  46.0 1.1 %copy.17 = bf16[1536,512]{1,0:T(8,128)(2,1)} copy(bf16[1536,512]{1,0:T(8,128)(2,1)S(1)} %get-tuple-element.4) | data formatting | bytes 3145728
  47.1 0.7 %copy.18 = bf16[128,512]{1,0:T(8,128)(2,1)} copy(bf16[128,512]{1,0:T(8,128)(2,1)S(1)} %get-tuple-element.5) | data formatting | bytes 262144
Async XLA Ops:
  0.6 1.4 %copy-start = (bf16[1536,512]{1,0:T(8,128)(2,1)S(1)}, bf16[1536,512]{1,0:T(8,128)(2,1)}, u32[]{:S(2)}) copy-start(bf16[1536,512]{1,0:T(8,128)(2,1)} %edges_hbm.1) | copy-start | bytes 4718596
  2.0 1.4 %copy-start.1 = (bf16[1536,512]{1,0:T(8,128)(2,1)S(1)}, bf16[1536,512]{1,0:T(8,128)(2,1)}, u32[]{:S(2)}) copy-start(bf16[1536,512]{1,0:T(8,128)(2,1)} %cot_hbm.1) | copy-start | bytes 4718596
  3.5 0.9 %copy-start.2 = (bf16[128,512]{1,0:T(8,128)(2,1)S(1)}, bf16[128,512]{1,0:T(8,128)(2,1)}, u32[]{:S(2)}) copy-start(bf16[128,512]{1,0:T(8,128)(2,1)} %nodes_hbm.1) | copy-start | bytes 393220
  4.4 0.9 %copy-start.3 = (bf16[128,512]{1,0:T(8,128)(2,1)S(1)}, bf16[128,512]{1,0:T(8,128)(2,1)}, u32[]{:S(2)}) copy-start(bf16[128,512]{1,0:T(8,128)(2,1)} %ncot_hbm.1) | copy-start | bytes 393220
  5.3 0.8 %copy-start.4 = (bf16[64,512]{1,0:T(8,128)(2,1)S(1)}, bf16[64,512]{1,0:T(8,128)(2,1)}, u32[]{:S(2)}) copy-start(bf16[64,512]{1,0:T(8,128)(2,1)} %wout_hbm.1) | copy-start | bytes 196612
  6.1 0.8 %copy-start.5 = (bf16[64,512]{1,0:T(8,128)(2,1)S(1)}, bf16[64,512]{1,0:T(8,128)(2,1)}, u32[]{:S(2)}) copy-start(bf16[64,512]{1,0:T(8,128)(2,1)} %wedge_hbm.1) | copy-start | bytes 196612
  6.9 0.8 %copy-start.6 = (bf16[64,512]{1,0:T(8,128)(2,1)S(1)}, bf16[64,512]{1,0:T(8,128)(2,1)}, u32[]{:S(2)}) copy-start(bf16[64,512]{1,0:T(8,128)(2,1)} %wsend_hbm.1) | copy-start | bytes 196612
  7.8 0.8 %copy-start.7 = (bf16[64,512]{1,0:T(8,128)(2,1)S(1)}, bf16[64,512]{1,0:T(8,128)(2,1)}, u32[]{:S(2)}) copy-start(bf16[64,512]{1,0:T(8,128)(2,1)} %wrecv_hbm.1) | copy-start | bytes 196612
  8.6 0.7 %copy-start.8 = (s32[1536]{0:T(1024)S(1)}, s32[1536]{0:T(1024)}, u32[]{:S(2)}) copy-start(s32[1536]{0:T(1024)} %param.17) | copy-start | bytes 18436
  9.3 0.7 %copy-start.9 = (s32[1536]{0:T(1024)S(1)}, s32[1536]{0:T(1024)}, u32[]{:S(2)}) copy-start(s32[1536]{0:T(1024)} %param.18) | copy-start | bytes 18436
  10.0 0.7 %copy-start.10 = (f32[512]{0:T(512)S(1)}, f32[512]{0:T(512)}, u32[]{:S(2)}) copy-start(f32[512]{0:T(512)} %param.25) | copy-start | bytes 6148
  10.7 0.7 %copy-start.11 = (s32[12]{0:T(128)S(1)}, s32[12]{0:T(128)}, u32[]{:S(2)}) copy-start(s32[12]{0:T(128)} %slots_ref.1) | copy-start | bytes 148
  11.4 0.7 %copy-start.12 = (s32[12]{0:T(128)S(1)}, s32[12]{0:T(128)}, u32[]{:S(2)}) copy-start(s32[12]{0:T(128)} %live_ref.1) | copy-start | bytes 148

commit v2 on v1

--- a/solution.py
+++ b/solution.py
@@ -23,11 +23,11 @@
 
 def kernel(
     cfg,
-    slots_ref,
-    live_ref,
-    senders_ref,
-    receivers_ref,
-    bias_ref,
+    slots_hbm,
+    live_hbm,
+    senders_hbm,
+    receivers_hbm,
+    bias_hbm,
     nodes_hbm,
     edges_hbm,
     cot_hbm,
@@ -36,8 +36,13 @@
     wedge_hbm,
     wsend_hbm,
     wrecv_hbm,
-    gedges_hbm,
+    gedges_ref,
     gnodes_ref,
+    slots_ref,
+    live_ref,
+    senders_ref,
+    receivers_ref,
+    bias_ref,
     wall,
     table,
     edges_v,
@@ -50,12 +55,9 @@
     pre,
     proj,
     gpre,
-    sums,
     back_out,
     back_in,
-    out_v,
     local_sem,
-    out_sem,
     send_sem,
     recv_sem,
 ):
@@ -80,7 +82,14 @@
     ncot_copy = local(ncot_hbm, ncot_v, 5)
     cot_copy = local(cot_hbm, cot_v, 6)
     edges_copy = local(edges_hbm, edges_v, 7)
-    for copy in [nodes_copy] + w_copies + [ncot_copy, cot_copy, edges_copy]:
+    small_copies = [
+        local(slots_hbm, slots_ref, 8),
+        local(live_hbm, live_ref, 9),
+        local(senders_hbm, senders_ref, 10),
+        local(receivers_hbm, receivers_ref, 11),
+        local(bias_hbm, bias_ref, 12),
+    ]
+    for copy in [nodes_copy] + w_copies + small_copies + [ncot_copy, cot_copy, edges_copy]:
         copy.start()
 
     right = (ens, (bx + 1) % n_bx, by)
@@ -206,8 +215,8 @@
         a_x = [to_x(part_a, 0)]
         b_z = z_sends(part_b)
         b_x = [to_x(part_b, 0)]
-    ncot_copy.wait()
-    cot_copy.wait()
+    for copy in small_copies + [ncot_copy, cot_copy]:
+        copy.wait()
     prepare(0, third)
     a_y, a_c, a_c2, b_c = [], [], [], []
     if gather:
@@ -264,8 +273,7 @@
         slope = sigma * (1.0 + act * (1.0 - sigma))
         gpre[here, :] = (gact[here, :] * slope).astype(jnp.bfloat16)
 
-    sums[...] = dot(oht[...], gpre[...])
-    back_out[...] = sums[pl.ds(node_dev, node_dev), :].astype(jnp.bfloat16)
+    back_out[...] = dot(oht[pl.ds(node_dev, node_dev), :], gpre[...]).astype(jnp.bfloat16)
     backs = [(rim, left), (rim, right), (rim, core), (COARSE, far[0]), (COARSE, far[1])]
     back_msgs = []
     place = 0
@@ -274,22 +282,20 @@
         back_msgs.append(message(back_out.at[here], back_in.at[here], device, back_in.at[here]))
         place += size
 
-    outs = []
-    for number in range(rows // chunk):
-        here = pl.ds(number * chunk, chunk)
-        out_v[here, :] = (
+    @pl.loop(0, rows // chunk)
+    def _(number):
+        here = pl.ds(pl.multiple_of(number * chunk, chunk), chunk)
+        gedges_ref[here, :] = (
             cot_v[here, :].astype(jnp.float32) + dot(gpre[here, :], weight(1), NT)
         ).astype(jnp.bfloat16)
-        copy = pltpu.make_async_copy(out_v.at[here], gedges_hbm.at[here], out_sem.at[number])
-        copy.start()
-        outs.append(copy)
-
-    received = dot(
-        sums[pl.ds(2 * node_dev, node_dev), :].astype(jnp.bfloat16), weight(3), NT
-    ) + ncot_v[...].astype(jnp.float32)
+
+    own = dot(oht[pl.ds(0, node_dev), :], gpre[...])
+    received = dot(oht[pl.ds(2 * node_dev, node_dev), :], gpre[...])
+    received = dot(received.astype(jnp.bfloat16), weight(3), NT) + ncot_v[...].astype(
+        jnp.float32
+    )
     for arrival in back_msgs:
         arrival.wait_recv()
-    own = sums[pl.ds(0, node_dev), :]
     got = back_in[...].astype(jnp.float32)
     coarse = got[3 * rim : 3 * rim + COARSE] + got[3 * rim + COARSE :]
     low = own[:rim] + got[rim : 2 * rim]
@@ -302,7 +308,19 @@
     )
     for copy in sent:
         copy.wait_send()
-    for copy in outs:
+
+
+def write_out(edges_ref, nodes_ref, edges_hbm, nodes_hbm, sem):
+    quarter = edges_ref.shape[0] // 4
+    copies = [pltpu.make_async_copy(nodes_ref, nodes_hbm, sem.at[4])]
+    for number in range(4):
+        here = pl.ds(number * quarter, quarter)
+        copies.append(
+            pltpu.make_async_copy(edges_ref.at[here], edges_hbm.at[here], sem.at[number])
+        )
+    for copy in copies:
+        copy.start()
+    for copy in copies:
         copy.wait()
 
 
@@ -338,18 +356,22 @@
     bf16, f32 = jnp.bfloat16, jnp.float32
     wall = (4, nz, 2, shard_rows, width) if gather else (4, depth, width)
     count = 3 * nz + 64
-    smem = pl.BlockSpec(memory_space=pltpu.SMEM)
     vmem = pl.BlockSpec(memory_space=pltpu.VMEM)
     hbm = pl.BlockSpec(memory_space=pl.ANY)
-    return pl.pallas_call(
+    results = pl.pallas_call(
         functools.partial(kernel, cfg),
         out_shape=(
-            jax.ShapeDtypeStruct((rows, width), bf16),
-            jax.ShapeDtypeStruct((node_dev, width), bf16),
+            pltpu.VMEM((rows, width), bf16),
+            pltpu.VMEM((node_dev, width), bf16),
         ),
-        in_specs=[smem, smem, vmem, vmem, vmem] + [hbm] * 8,
-        out_specs=(hbm, vmem),
+        in_specs=[hbm] * 13,
+        out_specs=(vmem, vmem),
         scratch_shapes=[
+            pltpu.SMEM((blocks,), jnp.int32),
+            pltpu.SMEM((blocks,), jnp.int32),
+            pltpu.VMEM((blocks, block), jnp.int32),
+            pltpu.VMEM((blocks, block), jnp.int32),
+            pltpu.VMEM((1, width), f32),
             pltpu.VMEM(wall, bf16),
             pltpu.VMEM((2 * node_dev, width), bf16),
             pltpu.VMEM((rows, width), bf16),
@@ -362,17 +384,14 @@
             pltpu.VMEM((rows, width), f32),
             pltpu.VMEM((3 * node_dev, width), bf16),
             pltpu.VMEM((rows, width), bf16),
-            pltpu.VMEM((3 * node_dev, width), f32),
             pltpu.VMEM((node_dev, width), bf16),
             pltpu.VMEM((node_dev, width), bf16),
-            pltpu.VMEM((rows, width), bf16),
-            pltpu.SemaphoreType.DMA((8,)),
-            pltpu.SemaphoreType.DMA((rows // chunk,)),
+            pltpu.SemaphoreType.DMA((13,)),
             pltpu.SemaphoreType.DMA((count,)),
             pltpu.SemaphoreType.DMA((count,)),
         ],
         compiler_params=pltpu.CompilerParams(
-            collective_id=0, has_side_effects=True, vmem_limit_bytes=48 * 1024 * 1024
+            collective_id=0, has_side_effects=True, vmem_limit_bytes=60 * 1024 * 1024
         ),
     )(
         slots,
@@ -386,6 +405,17 @@
         node_cotangent,
         *weights,
     )
+    return pl.pallas_call(
+        write_out,
+        out_shape=(
+            jax.ShapeDtypeStruct((rows, width), bf16),
+            jax.ShapeDtypeStruct((node_dev, width), bf16),
+        ),
+        in_specs=[vmem, vmem],
+        out_specs=(hbm, hbm),
+        scratch_shapes=[pltpu.SemaphoreType.DMA((5,))],
+        compiler_params=pltpu.CompilerParams(vmem_limit_bytes=1024 * 1024),
+    )(*results)
 
 
 def solution(mesh):

time: 48.3 us -> 34.3 us (0.71)
  local copies, waits for them, and re-layouts: 13.2 us -> 0 us
  Pallas kernels: 34 us -> 33.5 us
    unnamed x28 -> x0, local copies, waits for them, and re-layouts: 13.2 us -> none
    pallas_call x1 -> x2, Pallas kernels: 34 us -> 33.5 us  [the longest x1 32.3 us: per_device(): pl.pallas_call(functools.partial(kernel, cfg), out_shape=(pltpu.VMEM((row...]
where the time goes in v2:
time: 34.3 us; the launch traced here: 34.1 us
  Pallas kernels  33.5 us (98%)
  between operations  0.64 us (2%)
    pallas_call x1, Pallas kernels, per_device(): pl.pallas_call(functools.partial(kernel, cfg), out_shape=(pltpu.VMEM((row...  32.3 us
    pallas_call x1, Pallas kernels, per_device(): pl.pallas_call(write_out, out_shape=(jax.ShapeDtypeStruct((rows, width),...  1.22 us

profile of v2, /device:TPU:0, one launch (start us, length us, event | category | flops | bytes accessed | tf_op | source)
XLA Modules:
  0.0 34.1 jit_solution(5354846628611542143)
XLA Ops:
  0.6 32.3 %shard_map.140 = (bf16[1536,512]{1,0:T(8,128)(2,1)S(1)}, bf16[128,512]{1,0:T(8,128)(2,1)S(1)}) custom-call(s32[12]{0:T(128)} %slots_hbm.1, s32[12]{0:T(128)} %live_hbm.1, s32[12,128]{1,0:T(8,128)} %bitcast.3, s32[12,128]{1,0:T(8,128)} %bitcast.4, f32[1,512]{1,0:T(1,128)} %bitcast.5, bf16[128,512]{1,0:T(8,128)(2,1)} %nodes_hbm.1, ...), custom_call_target="tpu_custom_call" | custom-call | tf_op jit(solution)/shard_map/pallas_call | solution.py:361
  32.9 1.2 %shard_map.141 = (bf16[1536,512]{1,0:T(8,128)(2,1)}, bf16[128,512]{1,0:T(8,128)(2,1)}) custom-call(bf16[1536,512]{1,0:T(8,128)(2,1)S(1)} %get-tuple-element.4.edges_ref, bf16[128,512]{1,0:T(8,128)(2,1)S(1)} %get-tuple-element.5.nodes_ref), custom_call_target="tpu_custom_call" | custom-call | tf_op jit(solution)/shard_map/pallas_call | solution.py:408

commit v3 on v2

--- a/solution.py
+++ b/solution.py
@@ -141,33 +141,36 @@
         (0, COARSE, far[0]),
         (0, COARSE, far[1]),
     ]
-    node_msgs = []
-    place = node_dev
-    for start, size, device in pieces:
-        target = table.at[pl.ds(place, size)]
-        node_msgs.append(message(table.at[pl.ds(start, size)], target, device, target))
-        place += size
+    shared = 2
 
     def part_a(zz, xx, e, b):
         size = shard_rows // 4
         start = pl.multiple_of((2 * e + b) * size, size)
-        return wall.at[pl.ds(0, 2), zz, xx, pl.ds(start, size)]
+        return wall.at[pl.ds(0, shared), zz, xx, pl.ds(start, size)]
 
     def part_b(zz, xx, e, b):
         size = shard_rows // 2
         start = pl.multiple_of(b * size, size)
-        return wall.at[pl.ds(2, 2), zz, xx, pl.ds(start, size)]
+        return wall.at[pl.ds(shared, 4 - shared), zz, xx, pl.ds(start, size)]
+
+    def other(step):
+        out = z
+        if step & 1:
+            out = flip(out, 1)
+        if step & 2:
+            out = flip(out, 2)
+        return out
 
     def z_sends(part):
         got = []
         own = part(z, x, ens, by)
         for dz in range(1, nz):
-            incoming = part((z - dz + nz) % nz, x, ens, by)
-            got.append(message(own, own, (ens, ((z + dz) % nz) * 2 + x, by), incoming))
+            incoming = part(other(dz), x, ens, by)
+            got.append(message(own, own, (ens, other(dz) * 2 + x, by), incoming))
         return got
 
     def forward(part, dz, xx, e, b, device, arrives):
-        zz = (z - dz + nz) % nz
+        zz = other(dz)
         source = part(zz, xx, e, b)
         return message(source, source, device, part(zz, *arrives))
 
@@ -213,6 +216,13 @@
     if gather:
         a_z = z_sends(part_a)
         a_x = [to_x(part_a, 0)]
+    node_msgs = []
+    place = node_dev
+    for start, size, device in pieces:
+        target = table.at[pl.ds(place, size)]
+        node_msgs.append(message(table.at[pl.ds(start, size)], target, device, target))
+        place += size
+    if gather:
         b_z = z_sends(part_b)
         b_x = [to_x(part_b, 0)]
     for copy in small_copies + [ncot_copy, cot_copy]:
@@ -252,12 +262,6 @@
 
     edges_copy.wait()
 
-    @pl.loop(0, rows // chunk)
-    def _(number):
-        here = pl.ds(pl.multiple_of(number * chunk, chunk), chunk)
-        gact[here, :] = dot(gmsg[here, :], weight(0), NT)
-        pre[here, :] = dot(edges_v[here, :], weight(1)) + bias_ref[...]
-
     for arrival in b_c + node_msgs:
         arrival.wait_recv()
     proj[pl.ds(0, 2 * node_dev), :] = dot(table[...], weight(2)).astype(jnp.bfloat16)
@@ -265,13 +269,12 @@
         table[pl.ds(0, node_dev), :], weight(3)
     ).astype(jnp.bfloat16)
 
-    @pl.loop(0, rows // chunk)
-    def _(number):
-        here = pl.ds(pl.multiple_of(number * chunk, chunk), chunk)
-        act = pre[here, :] + dot(oh[here, :], proj[...])
+    for number in range(rows // chunk):
+        here = pl.ds(number * chunk, chunk)
+        act = dot(edges_v[here, :], weight(1)) + dot(oh[here, :], proj[...]) + bias_ref[...]
         sigma = 0.5 + 0.5 * jnp.tanh(0.5 * act)
         slope = sigma * (1.0 + act * (1.0 - sigma))
-        gpre[here, :] = (gact[here, :] * slope).astype(jnp.bfloat16)
+        gpre[here, :] = (dot(gmsg[here, :], weight(0), NT) * slope).astype(jnp.bfloat16)
 
     back_out[...] = dot(oht[pl.ds(node_dev, node_dev), :], gpre[...]).astype(jnp.bfloat16)
     backs = [(rim, left), (rim, right), (rim, core), (COARSE, far[0]), (COARSE, far[1])]

time: 34.3 us -> 31 us (0.904)
  Pallas kernels: 33.5 us -> 30.2 us
    pallas_call x1, Pallas kernels: 32.3 us -> 29 us  [per_device(): pl.pallas_call(functools.partial(kernel, cfg), out_shape=(pltpu.VMEM((row...]
where the time goes in v3:
time: 31 us; the launch traced here: 30.8 us
  Pallas kernels  30.2 us (97%)
  between operations  0.64 us (2%)
    pallas_call x1, Pallas kernels, per_device(): pl.pallas_call(functools.partial(kernel, cfg), out_shape=(pltpu.VMEM((row...  29 us
    pallas_call x1, Pallas kernels, per_device(): pl.pallas_call(write_out, out_shape=(jax.ShapeDtypeStruct((rows, width),...  1.22 us

profile of v3, /device:TPU:0, one launch (start us, length us, event | category | flops | bytes accessed | tf_op | source)
XLA Modules:
  0.0 30.8 jit_solution(11430123231993641885)
XLA Ops:
  0.6 29.0 %shard_map.140 = (bf16[1536,512]{1,0:T(8,128)(2,1)S(1)}, bf16[128,512]{1,0:T(8,128)(2,1)S(1)}) custom-call(s32[12]{0:T(128)} %slots_hbm.1, s32[12]{0:T(128)} %live_hbm.1, s32[12,128]{1,0:T(8,128)} %bitcast.3, s32[12,128]{1,0:T(8,128)} %bitcast.4, f32[1,512]{1,0:T(1,128)} %bitcast.5, bf16[128,512]{1,0:T(8,128)(2,1)} %nodes_hbm.1, ...), custom_call_target="tpu_custom_call" | custom-call | tf_op jit(solution)/shard_map/pallas_call | solution.py:364
  29.6 1.2 %shard_map.141 = (bf16[1536,512]{1,0:T(8,128)(2,1)}, bf16[128,512]{1,0:T(8,128)(2,1)}) custom-call(bf16[1536,512]{1,0:T(8,128)(2,1)S(1)} %get-tuple-element.4.edges_ref, bf16[128,512]{1,0:T(8,128)(2,1)S(1)} %get-tuple-element.5.nodes_ref), custom_call_target="tpu_custom_call" | custom-call | tf_op jit(solution)/shard_map/pallas_call | solution.py:411

commit v4 on v3

--- a/solution.py
+++ b/solution.py
@@ -70,6 +70,20 @@
     ens, bx, by = lax.axis_index("ens"), lax.axis_index("bx"), lax.axis_index("by")
     z, x = bx // 2, bx % 2
 
+    right = (ens, (bx + 1) % n_bx, by)
+    left = (ens, (bx + n_bx - 1) % n_bx, by)
+    core = (ens, bx, 1 - by)
+    far = [(ens, flip(bx, n_bx // 2), by), (ens, flip(bx, n_bx // 4), by)]
+    x_peer = (ens, z * 2 + 1 - x, by)
+    y_peer = (1 - ens, bx, by)
+    greeted = [right, left, core] + far
+    if gather:
+        greeted += [(ens, ((z + dz) % nz) * 2 + x, by) for dz in range(1, nz)]
+        greeted += [x_peer, y_peer]
+
+    barrier = pltpu.get_barrier_semaphore()
+    for device in greeted:
+        pl.semaphore_signal(barrier, inc=1, device_id=device, device_id_type=MESH)
     def local(source, target, number):
         return pltpu.make_async_copy(source, target, local_sem.at[number])
 
@@ -89,23 +103,9 @@
         local(receivers_hbm, receivers_ref, 11),
         local(bias_hbm, bias_ref, 12),
     ]
-    for copy in [nodes_copy] + w_copies + small_copies + [ncot_copy, cot_copy, edges_copy]:
+    for copy in w_copies + [nodes_copy] + small_copies + [ncot_copy, cot_copy, edges_copy]:
         copy.start()
 
-    right = (ens, (bx + 1) % n_bx, by)
-    left = (ens, (bx + n_bx - 1) % n_bx, by)
-    core = (ens, bx, 1 - by)
-    far = [(ens, flip(bx, n_bx // 2), by), (ens, flip(bx, n_bx // 4), by)]
-    x_peer = (ens, z * 2 + 1 - x, by)
-    y_peer = (1 - ens, bx, by)
-    greeted = [right, left, core] + far
-    if gather:
-        greeted += [(ens, ((z + dz) % nz) * 2 + x, by) for dz in range(1, nz)]
-        greeted += [x_peer, y_peer]
-
-    barrier = pltpu.get_barrier_semaphore()
-    for device in greeted:
-        pl.semaphore_signal(barrier, inc=1, device_id=device, device_id_type=MESH)
     pl.semaphore_wait(barrier, len(greeted))
 
     used = [0]
@@ -216,15 +216,14 @@
     if gather:
         a_z = z_sends(part_a)
         a_x = [to_x(part_a, 0)]
+        b_z = z_sends(part_b)
+        b_x = [to_x(part_b, 0)]
     node_msgs = []
     place = node_dev
     for start, size, device in pieces:
         target = table.at[pl.ds(place, size)]
         node_msgs.append(message(table.at[pl.ds(start, size)], target, device, target))
         place += size
-    if gather:
-        b_z = z_sends(part_b)
-        b_x = [to_x(part_b, 0)]
     for copy in small_copies + [ncot_copy, cot_copy]:
         copy.wait()
     prepare(0, third)
@@ -240,15 +239,17 @@
             a_x[dz].wait_recv()
             a_y.append((dz, 1 - x, to_y(part_a, dz, 1 - x)))
             a_c.append(to_core(part_a, dz, 1 - x, ens))
-        for dz in range(1, nz):
-            b_z[dz - 1].wait_recv()
-            b_x.append(to_x(part_b, dz))
-            b_c.append(to_core(part_b, dz, x, ens))
+            if dz:
+                b_z[dz - 1].wait_recv()
+                b_x.append(to_x(part_b, dz))
+                b_c.append(to_core(part_b, dz, x, ens))
         prepare(2 * third, blocks)
-        for dz, xx, arrival in a_y:
+        for dz, xx, arrival in a_y[: nz - 1]:
             arrival.wait_recv()
             a_c2.append(to_core(part_a, dz, xx, 1 - ens))
-        for dz in range(nz):
+        for dz, xx, arrival in a_y[nz - 1 :]:
+            arrival.wait_recv()
+            a_c2.append(to_core(part_a, dz, xx, 1 - ens))
             b_x[dz].wait_recv()
             b_c.append(to_core(part_b, dz, 1 - x, ens))
         for arrival in a_c + a_c2:
@@ -297,6 +298,8 @@
     received = dot(received.astype(jnp.bfloat16), weight(3), NT) + ncot_v[...].astype(
         jnp.float32
     )
+    for copy in sent:
+        copy.wait_send()
     for arrival in back_msgs:
         arrival.wait_recv()
     got = back_in[...].astype(jnp.float32)
@@ -309,8 +312,6 @@
     gnodes_ref[...] = (received + dot(own.astype(jnp.bfloat16), weight(2), NT)).astype(
         jnp.bfloat16
     )
-    for copy in sent:
-        copy.wait_send()
 
 
 def write_out(edges_ref, nodes_ref, edges_hbm, nodes_hbm, sem):

time: 31 us -> 30.5 us (0.984)
  Pallas kernels: 30.2 us -> 29.6 us
    pallas_call x1, Pallas kernels: 29 us -> 28.4 us  [per_device(): pl.pallas_call(functools.partial(kernel, cfg), out_shape=(pltpu.VMEM((row...]
where the time goes in v4:
time: 30.5 us; the launch traced here: 30.3 us
  Pallas kernels  29.6 us (97%)
  between operations  0.64 us (2%)
    pallas_call x1, Pallas kernels, per_device(): pl.pallas_call(functools.partial(kernel, cfg), out_shape=(pltpu.VMEM((row...  28.4 us
    pallas_call x1, Pallas kernels, per_device(): pl.pallas_call(write_out, out_shape=(jax.ShapeDtypeStruct((rows, width),...  1.22 us

profile of v4, /device:TPU:0, one launch (start us, length us, event | category | flops | bytes accessed | tf_op | source)
XLA Modules:
  0.0 30.3 jit_solution(725641892520892158)
XLA Ops:
  0.6 28.4 %shard_map.140 = (bf16[1536,512]{1,0:T(8,128)(2,1)S(1)}, bf16[128,512]{1,0:T(8,128)(2,1)S(1)}) custom-call(s32[12]{0:T(128)} %slots_hbm.1, s32[12]{0:T(128)} %live_hbm.1, s32[12,128]{1,0:T(8,128)} %bitcast.3, s32[12,128]{1,0:T(8,128)} %bitcast.4, f32[1,512]{1,0:T(1,128)} %bitcast.5, bf16[128,512]{1,0:T(8,128)(2,1)} %nodes_hbm.1, ...), custom_call_target="tpu_custom_call" | custom-call | tf_op jit(solution)/shard_map/pallas_call | solution.py:365
  29.0 1.2 %shard_map.141 = (bf16[1536,512]{1,0:T(8,128)(2,1)}, bf16[128,512]{1,0:T(8,128)(2,1)}) custom-call(bf16[1536,512]{1,0:T(8,128)(2,1)S(1)} %get-tuple-element.4.edges_ref, bf16[128,512]{1,0:T(8,128)(2,1)S(1)} %get-tuple-element.5.nodes_ref), custom_call_target="tpu_custom_call" | custom-call | tf_op jit(solution)/shard_map/pallas_call | solution.py:412

commit v5 on v4

--- a/solution.py
+++ b/solution.py
@@ -183,6 +183,15 @@
     def to_core(part, dz, xx, e):
         return forward(part, dz, xx, e, by, core, (xx, e, 1 - by))
 
+    def column_to_core(xx, e):
+        size = shard_rows // 4
+
+        def column(b):
+            start = pl.multiple_of((2 * e + b) * size, size)
+            return wall.at[pl.ds(0, shared), :, xx, pl.ds(start, size)]
+
+        return message(column(by), column(by), core, column(1 - by))
+
     def prepare(first, last):
         @pl.loop(first, last)
         def _(number):
@@ -238,18 +247,18 @@
         for dz in range(nz):
             a_x[dz].wait_recv()
             a_y.append((dz, 1 - x, to_y(part_a, dz, 1 - x)))
-            a_c.append(to_core(part_a, dz, 1 - x, ens))
-            if dz:
-                b_z[dz - 1].wait_recv()
-                b_x.append(to_x(part_b, dz))
-                b_c.append(to_core(part_b, dz, x, ens))
+        a_c.append(column_to_core(1 - x, ens))
+        for dz in range(1, nz):
+            b_z[dz - 1].wait_recv()
+            b_x.append(to_x(part_b, dz))
+            b_c.append(to_core(part_b, dz, x, ens))
         prepare(2 * third, blocks)
-        for dz, xx, arrival in a_y[: nz - 1]:
+        for dz, xx, arrival in a_y:
             arrival.wait_recv()
-            a_c2.append(to_core(part_a, dz, xx, 1 - ens))
-        for dz, xx, arrival in a_y[nz - 1 :]:
-            arrival.wait_recv()
-            a_c2.append(to_core(part_a, dz, xx, 1 - ens))
+            if dz and xx is x:
+                a_c2.append(to_core(part_a, dz, xx, 1 - ens))
+        a_c2.append(column_to_core(1 - x, 1 - ens))
+        for dz in range(nz):
             b_x[dz].wait_recv()
             b_c.append(to_core(part_b, dz, 1 - x, ens))
         for arrival in a_c + a_c2:

time: 30.5 us -> 30.5 us (level)
  no operation moved by 1% of the time
where the time goes in v5:
time: 30.5 us; the launch traced here: 30.3 us
  Pallas kernels  29.7 us (97%)
  between operations  0.64 us (2%)
    pallas_call x1, Pallas kernels, per_device(): pl.pallas_call(functools.partial(kernel, cfg), out_shape=(pltpu.VMEM((row...  28.4 us
    pallas_call x1, Pallas kernels, per_device(): pl.pallas_call(write_out, out_shape=(jax.ShapeDtypeStruct((rows, width),...  1.22 us

profile of v5, /device:TPU:0, one launch (start us, length us, event | category | flops | bytes accessed | tf_op | source)
XLA Modules:
  0.0 30.3 jit_solution(5554144294845370344)
XLA Ops:
  0.6 28.4 %shard_map.140 = (bf16[1536,512]{1,0:T(8,128)(2,1)S(1)}, bf16[128,512]{1,0:T(8,128)(2,1)S(1)}) custom-call(s32[12]{0:T(128)} %slots_hbm.1, s32[12]{0:T(128)} %live_hbm.1, s32[12,128]{1,0:T(8,128)} %bitcast.3, s32[12,128]{1,0:T(8,128)} %bitcast.4, f32[1,512]{1,0:T(1,128)} %bitcast.5, bf16[128,512]{1,0:T(8,128)(2,1)} %nodes_hbm.1, ...), custom_call_target="tpu_custom_call" | custom-call | tf_op jit(solution)/shard_map/pallas_call | solution.py:374
  29.1 1.2 %shard_map.141 = (bf16[1536,512]{1,0:T(8,128)(2,1)}, bf16[128,512]{1,0:T(8,128)(2,1)}) custom-call(bf16[1536,512]{1,0:T(8,128)(2,1)S(1)} %get-tuple-element.4.edges_ref, bf16[128,512]{1,0:T(8,128)(2,1)S(1)} %get-tuple-element.5.nodes_ref), custom_call_target="tpu_custom_call" | custom-call | tf_op jit(solution)/shard_map/pallas_call | solution.py:421
